TPU v7x, 32 devices: a whole 2x2x4 slice. The times are simulated.
32 devices in a mesh: grp: 8 (over z, x), intra: 4 (over y, core).
Axes of the slice: x: 2, y: 2, z: 4, core: 2. Of those that a mesh axis runs over, the one named last changes fastest.
Arguments:
- normed: bfloat16 [4096, 4096], P(('grp', 'intra')), may hold values from -6 to 6
- cotangent: bfloat16 [4096, 1024], P(('grp', 'intra')), may hold values from -0.09375 to 0.09375
- norm_gain: float32 [4096], replicated, may hold values from 0.25 to 4
- weights: bfloat16 [4096, 1024], P('intra'), may hold values from -6 to 6
- row_state: float32 [8, 4, 86, 16], P('grp', 'intra'), may hold values from 0.05 to 20
- col_state: float32 [8, 128], replicated, may hold values from 0.3 to 10
- owner_table: int32 [512, 1], replicated, may hold values from 0 to 7; in each aligned block of 512 rows (0 to 511, 512 to 1023, ...) at most 86 rows name the same one
Outputs:
- new_weights: bfloat16 [4096, 1024], P('intra')
- row_moments: float32 [8, 4, 86, 16], P('grp', 'intra')
- col_moments: float32 [8, 128], replicated
Inputs may be any that keep to these rules, and one draw needn't show every extreme that they name: `owner_table`: each group owns at most 86 units, some group exactly 86, and every group owns at least one.
All inputs are finite; a program needn't handle non-finite values.
Results may differ from a plain program's by a relative error of at most 0.013.
Values may be sent and summed in bfloat16 or wider, within the bound.
A program may use at most 64 MiB of HBM per device.

v0:
```python
import jax
import jax.numpy as jnp
from jax import lax
from jax.sharding import PartitionSpec as P

decay_rate = 0.8
step_size = 0.5
epsilon = 1e-06


def to_units(block, blocks, unit_rows, tensors, head):
    return (
        block.reshape(blocks, unit_rows, tensors, head)
        .transpose(2, 0, 1, 3)
        .reshape(tensors * blocks, unit_rows, head)
    )


def from_units(units, blocks, unit_rows, tensors, head):
    return (
        units.reshape(tensors, blocks, unit_rows, head)
        .transpose(1, 2, 0, 3)
        .reshape(blocks * unit_rows, tensors * head)
    )


def on_device(normed, cotangent, norm_gain, weights, row_state, col_state, owner_table):
    groups = lax.axis_size("grp")
    members = lax.axis_size("intra")
    d_model = normed.shape[1]
    tokens_here = cotangent.shape[0]
    width = cotangent.shape[1]
    tensors = col_state.shape[0]
    head = col_state.shape[1]
    capacity = row_state.shape[2]
    unit_rows = row_state.shape[3]
    slab_rows = weights.shape[0]
    blocks = slab_rows // unit_rows
    unit_count = tensors * blocks
    scaled = (normed * norm_gain[None, :]).astype(jnp.bfloat16)
    columns = lax.all_to_all(scaled, "intra", split_axis=1, concat_axis=0, tiled=True)
    peer_grads = lax.all_gather(cotangent, "intra", axis=0, tiled=True)

    def add_term(total, pair):
        left, right = pair
        term = lax.dot_general(
            left, right, (((0,), (0,)), ((), ())), preferred_element_type=jnp.float32
        ).astype(jnp.bfloat16)
        term = lax.optimization_barrier(term)
        return (total + term.astype(jnp.float32), None)

    slab, _ = lax.scan(
        add_term,
        jnp.zeros((slab_rows, width), jnp.float32),
        (
            columns.reshape(members, tokens_here, slab_rows),
            peer_grads.reshape(members, tokens_here, width),
        ),
    )
    owner_flat = owner_table[:, 0]
    onehot = (owner_flat[:, None] == jnp.arange(groups, dtype=jnp.int32)[None, :]).astype(jnp.int32)
    before = jnp.cumsum(onehot, axis=0) - onehot
    slot = jnp.sum(before * onehot, axis=1)
    unit_ids = jnp.arange(unit_count, dtype=jnp.int32)
    matches = (owner_flat[None, None, :] == jnp.arange(groups, dtype=jnp.int32)[:, None, None]) & (
        slot[None, None, :] == jnp.arange(capacity, dtype=jnp.int32)[None, :, None]
    )
    filled = jnp.any(matches, axis=2)
    send_index = jnp.where(
        filled, jnp.sum(jnp.where(matches, unit_ids[None, None, :], 0), axis=2), unit_count
    )
    my_group = lax.axis_index("grp")
    my_index = lax.dynamic_index_in_dim(send_index, my_group, 0, keepdims=False)
    valid = my_index < unit_count
    weight_units = to_units(weights, blocks, unit_rows, tensors, head)
    weight_padded = jnp.concatenate(
        [weight_units, jnp.zeros((1, unit_rows, head), weights.dtype)], axis=0
    )
    grad_units = to_units(slab, blocks, unit_rows, tensors, head)
    grad_padded = jnp.concatenate(
        [grad_units, jnp.zeros((1, unit_rows, head), jnp.float32)], axis=0
    )
    outgoing = jnp.take(grad_padded, send_index.reshape(-1), axis=0).reshape(
        groups, capacity, unit_rows, head
    )
    incoming = lax.all_to_all(
        outgoing.astype(jnp.bfloat16), "grp", split_axis=0, concat_axis=0, tiled=True
    ).astype(outgoing.dtype)
    grad_own = jnp.sum(incoming, axis=0)
    own_weights = jnp.take(weight_padded, my_index, axis=0)
    tensor_hot = (
        (my_index // blocks)[:, None] == jnp.arange(tensors, dtype=jnp.int32)[None, :]
    ).astype(jnp.float32)
    squares = grad_own * grad_own
    row_mean = jnp.mean(squares, axis=2) + epsilon
    row_new = jnp.where(
        valid[:, None], decay_rate * row_state[0, 0] + (1.0 - decay_rate) * row_mean, 0.0
    )
    col_part = jnp.einsum("st,srh->th", tensor_hot, squares, precision=lax.Precision.HIGHEST)
    row_part = jnp.einsum("st,sr->t", tensor_hot, row_new, precision=lax.Precision.HIGHEST)
    col_total, row_total = lax.psum((col_part, row_part), ("grp", "intra"))
    col_new = decay_rate * col_state + (1.0 - decay_rate) * (col_total / d_model + epsilon)
    row_avg = row_total / d_model
    col_slot = jnp.dot(tensor_hot, col_new, precision=lax.Precision.HIGHEST)
    avg_slot = jnp.where(valid, jnp.dot(tensor_hot, row_avg, precision=lax.Precision.HIGHEST), 1.0)
    variance = row_new[:, :, None] * col_slot[:, None, :] / avg_slot[:, None, None]
    variance = jnp.where(valid[:, None, None], variance, 1.0)
    updated = (own_weights.astype(jnp.float32) - step_size * grad_own / jnp.sqrt(variance)).astype(
        jnp.bfloat16
    )
    collected = lax.all_gather(updated, "grp", axis=0, tiled=True)
    mine = jnp.take(collected, owner_flat * capacity + slot, axis=0)
    new_weights = from_units(mine, blocks, unit_rows, tensors, head)
    row_moments = row_new[None, None]
    return (new_weights, row_moments, col_new)


def solution(mesh):
    placed = (
        P(("grp", "intra"), None),
        P(("grp", "intra"), None),
        P(),
        P("intra", None),
        P("grp", "intra", None, None),
        P(),
        P(),
    )
    return jax.shard_map(
        on_device,
        mesh=mesh,
        in_specs=placed,
        out_specs=(P("intra", None), P("grp", "intra", None, None), P()),
        check_vma=False,
    )
```

profile of v0, /device:TPU:0, one launch (start us, length us, event | category | flops | bytes accessed | tf_op | source)
XLA Modules:
  0.0 261.0 jit_solution(12438313777037918329)
XLA Ops:
  7.2 1.6 copy.38
  8.8 1.5 multiply_convert_fusion
  10.3 4.2 %all-to-all-start = ((bf16[128,4,1024]{0,2,1:T(8,128)(2,1)}), bf16[128,4,1024]{0,2,1:T(8,128)(2,1)S(1)}, u32[]{:S(2)}, u32[]{:S(2)}) async-start(bf16[128,4,1024]{0,2,1:T(8,128)(2,1)} %bitcast.8), calls=%async_computation | async-start | bytes 2097152 | tf_op jit(solution)/shard_map/all_to_all | solution.py:41
  14.6 0.7 all-gather.3.cloned.1.call-update
  15.3 1.1 reduce-window.6
  16.4 0.2 slice_reduce_fusion
  16.9 1.6 and_reduce_fusion
  18.4 1.5 fusion.5
  20.3 8.7 %all-to-all-done = bf16[128,4,1024]{0,2,1:T(8,128)(2,1)S(1)} async-done(((bf16[128,4,1024]{0,2,1:T(8,128)(2,1)}), bf16[128,4,1024]{0,2,1:T(8,128)(2,1)S(1)}, u32[]{:S(2)}, u32[]{:S(2)}) %all-to-all-start) | async-done | bytes 1048608 | tf_op jit(solution)/shard_map/all_to_all | solution.py:41
  29.0 7.1 %all-gather.3.cloned.1.call-done = bf16[512,1024]{1,0:T(8,128)(2,1)} async-done(((bf16[128,1024]{1,0:T(8,128)(2,1)}), bf16[512,1024]{1,0:T(8,128)(2,1)}) %all-gather.3.cloned.1.call-update) | async-done | bytes 1048592 | tf_op jit(solution)/shard_map/all_gather | solution.py:42
  36.2 25.2 %while.11 = (s32[]{:T(128)}, f32[1024,1024]{1,0:T(8,128)}, bf16[4,128,1024]{1,2,0:T(8,128)(2,1)S(1)}, bf16[4,128,1024]{2,1,0:T(8,128)(2,1)}, s32[]{:T(128)}, /*index=5*/s32[]{:T(128)}) while((s32[]{:T(128)}, f32[1024,1024]{1,0:T(8,128)}, bf16[4,128,1024]{1,2,0:T(8,128)(2,1)S(1)}, bf16[4,128,1024]{2,1,0:T(8,128)(2,1)}, s32[]{:T(128)}, ...), condition=%wide.region_6.7_spmd.clone, body=%wide.region_5.6_spmd.clone.sunk | while | flops 272629760 | bytes 13108311 | solution.py:52
  36.2 1.6 convolution_convert_fusion.2
  37.8 3.0 %select_add_fusion.2 = f32[1024,1024]{1,0:T(8,128)} fusion(f32[1024,1024]{1,0:T(8,128)} %get-tuple-element.122, bf16[1024,1024]{1,0:T(8,128)(2,1)S(1)} %convolution_convert_fusion.2, pred[]{:T(512)S(6)} %compare.9), kind=kLoop, calls=%fused_computation.3.clone.1 | loop fusion | flops 3145728 | bytes 10485761 | tf_op jit(solution)/shard_map/while/body/eval_jaxpr/add | solution.py:50
  40.8 1.6 convolution_convert_fusion.2
  42.5 5.2 %select_add_fusion.2 = f32[1024,1024]{1,0:T(8,128)} fusion(f32[1024,1024]{1,0:T(8,128)} %get-tuple-element.122, bf16[1024,1024]{1,0:T(8,128)(2,1)S(1)} %convolution_convert_fusion.2, pred[]{:T(512)S(6)} %compare.9), kind=kLoop, calls=%fused_computation.3.clone.1 | loop fusion | flops 3145728 | bytes 10485761 | tf_op jit(solution)/shard_map/while/body/eval_jaxpr/add | solution.py:50
  47.7 1.6 convolution_convert_fusion.2
  49.3 5.2 %select_add_fusion.2 = f32[1024,1024]{1,0:T(8,128)} fusion(f32[1024,1024]{1,0:T(8,128)} %get-tuple-element.122, bf16[1024,1024]{1,0:T(8,128)(2,1)S(1)} %convolution_convert_fusion.2, pred[]{:T(512)S(6)} %compare.9), kind=kLoop, calls=%fused_computation.3.clone.1 | loop fusion | flops 3145728 | bytes 10485761 | tf_op jit(solution)/shard_map/while/body/eval_jaxpr/add | solution.py:50
  54.5 1.6 convolution_convert_fusion.2
  56.2 5.2 %select_add_fusion.2 = f32[1024,1024]{1,0:T(8,128)} fusion(f32[1024,1024]{1,0:T(8,128)} %get-tuple-element.122, bf16[1024,1024]{1,0:T(8,128)(2,1)S(1)} %convolution_convert_fusion.2, pred[]{:T(512)S(6)} %compare.9), kind=kLoop, calls=%fused_computation.3.clone.1 | loop fusion | flops 3145728 | bytes 10485761 | tf_op jit(solution)/shard_map/while/body/eval_jaxpr/add | solution.py:50
  61.4 3.2 %copy.47 = bf16[128,8,8,128]{3,2,1,0:T(8,128)(2,1)S(1)} copy(f32[128,8,8,128]{3,1,2,0:T(8,128)} %bitcast.78) | data formatting | bytes 6291456
  64.7 0.3 copy.40
  65.0 0.4 concatenate.7
  65.4 3.4 %gather_fusion.1 = bf16[688,16,128]{2,1,0:T(8,128)(2,1)} fusion(bf16[513,16,128]{2,1,0:T(8,128)(2,1)S(1)} %concatenate.7, s32[1024]{0:T(1024)S(1)} %pad_clamp_fusion.1), kind=kCustom, calls=%fused_computation.1 | custom fusion | bytes 5638848 | tf_op jit(solution)/shard_map/jit(_take)/gather | solution.py:83
  68.8 4.7 %select_convert_fusion = bf16[8,86,16,128]{3,2,1,0:T(8,128)(2,1)} fusion(bf16[8,86,16,128]{3,2,1,0:T(8,128)(2,1)} %bitcast.79, pred[8,86]{1,0:T(8,128)(4,1)S(1)} %copy.37), kind=kLoop, calls=%fused_computation.11 | loop fusion | flops 1409024 | bytes 5636784 | tf_op jit(solution)/shard_map/convert_element_type | solution.py:87
  73.5 6.6 %all-to-all-start.1 = ((bf16[8,86,16,128]{3,2,1,0:T(8,128)(2,1)}), bf16[8,86,16,128]{3,2,1,0:T(8,128)(2,1)S(1)}, u32[]{:S(2)}, u32[]{:S(2)}) async-start(bf16[8,86,16,128]{3,2,1,0:T(8,128)(2,1)} %select_convert_fusion), calls=%async_computation.1 | async-start | bytes 5636096 | tf_op jit(solution)/shard_map/all_to_all | solution.py:86
  80.2 0.7 copy.42
  80.9 2.2 copy.46
  83.1 0.2 bitcast_bitcast_fusion.1
  83.4 0.3 copy.36
  83.6 1.7 concatenate.6
  85.3 0.2 dynamic-slice_reduce_fusion
  85.6 58.6 %all-to-all-done.1 = bf16[8,86,16,128]{3,2,1,0:T(8,128)(2,1)S(1)} async-done(((bf16[8,86,16,128]{3,2,1,0:T(8,128)(2,1)}), bf16[8,86,16,128]{3,2,1,0:T(8,128)(2,1)S(1)}, u32[]{:S(2)}, u32[]{:S(2)}) %all-to-all-start.1) | async-done | bytes 2818080 | tf_op jit(solution)/shard_map/all_to_all | solution.py:86
  144.2 0.4 convert_reduce_fusion
  144.6 0.3 multiply_reduce_fusion
  145.0 0.2 fusion.23
  145.2 0.2 convolution_bitcast_fusion.1
  145.4 0.3 fusion.10
  145.6 2.3 gather_fusion
  147.9 37.9 %all-reduce.2 = (f32[8]{0:T(128)S(1)}, f32[8,128]{1,0:T(8,128)S(1)}) all-reduce(f32[8]{0:T(128)S(1)} %convolution_bitcast_fusion.1, f32[8,128]{1,0:T(8,128)S(1)} %fusion.10), channel_id=1, replica_groups=mesh['grp'=8,'intra'=4] {'grp','intra'}, use_global_device_ids=true, to_apply=%region_12.13 | all-reduce | flops 1032 | bytes 8256 | tf_op jit(solution)/shard_map/psum | solution.py:101
  185.8 0.2 fusion.6
  186.0 0.2 fusion.9
  186.3 1.8 subtract_convert_fusion
  188.3 0.7 copy.44
  189.0 56.8 %all-gather.5.cloned.1.call-done = bf16[688,16,128]{2,1,0:T(8,128)(2,1)} async-done(((bf16[86,16,128]{2,1,0:T(8,128)(2,1)}), bf16[688,16,128]{2,1,0:T(8,128)(2,1)}) %all-gather.5.cloned.1.call-update) | async-done | bytes 2818064 | tf_op jit(solution)/shard_map/all_gather | solution.py:111
  245.8 3.0 %gather_fusion.2 = bf16[512,16,128]{2,1,0:T(8,128)(2,1)S(1)} fusion(bf16[688,16,128]{2,1,0:T(8,128)(2,1)} %all-gather.5.cloned.1.call-done, s32[1024]{0:T(1024)S(1)} %pad_clamp_fusion), kind=kCustom, calls=%fused_computation.2 | custom fusion | bytes 4196352 | tf_op jit(solution)/shard_map/jit(_take)/gather | solution.py:112
  248.8 0.9 select_bitcast_fusion
  249.7 2.4 copy.43
  252.2 1.9 copy.50
  (40 shorter events, 1.1 us)
Async XLA Ops:
  7.2 1.6 copy-start.3
  8.8 6.5 %copy-start.2 = (s32[512,1]{0,1:T(1,128)S(1)}, s32[512,1]{0,1:T(1,128)}, u32[]{:S(2)}) copy-start(s32[512,1]{0,1:T(1,128)} %param.15) | copy-start | bytes 6148
  10.3 18.7 %all-to-all-start = ((bf16[128,4,1024]{0,2,1:T(8,128)(2,1)}), bf16[128,4,1024]{0,2,1:T(8,128)(2,1)S(1)}, u32[]{:S(2)}, u32[]{:S(2)}) async-start(bf16[128,4,1024]{0,2,1:T(8,128)(2,1)} %bitcast.8), calls=%async_computation | async-start | bytes 2097152 | tf_op jit(solution)/shard_map/all_to_all | solution.py:41
  14.6 21.6 %all-gather.3.cloned.1.call-start = ((), (), s32[]{:S(2)}) async-start(), calls=%async_computation.2 | async-start | bytes 1310720 | tf_op jit(solution)/shard_map/all_gather | solution.py:42
  73.5 6.7 %copy-start.4 = (f32[1,1,86,16]{2,3,1,0:T(8,128)S(1)}, f32[1,1,86,16]{2,3,1,0:T(8,128)}, u32[]{:S(2)}) copy-start(f32[1,1,86,16]{2,3,1,0:T(8,128)} %param.13) | copy-start | bytes 16516
  73.5 70.7 %all-to-all-start.1 = ((bf16[8,86,16,128]{3,2,1,0:T(8,128)(2,1)}), bf16[8,86,16,128]{3,2,1,0:T(8,128)(2,1)S(1)}, u32[]{:S(2)}, u32[]{:S(2)}) async-start(bf16[8,86,16,128]{3,2,1,0:T(8,128)(2,1)} %select_convert_fusion), calls=%async_computation.1 | async-start | bytes 5636096 | tf_op jit(solution)/shard_map/all_to_all | solution.py:86
  80.1 165.7 %all-gather.5.cloned.1.call-start = ((), (), s32[]{:S(2)}) async-start(), calls=%async_computation.3 | async-start | bytes 3170304 | tf_op jit(solution)/shard_map/all_gather | solution.py:111
  85.6 100.4 %copy-start.5 = (f32[8,128]{1,0:T(8,128)S(1)}, f32[8,128]{1,0:T(8,128)}, u32[]{:S(2)}) copy-start(f32[8,128]{1,0:T(8,128)} %param.14) | copy-start | bytes 12292
  144.2 0.8 copy-start
  144.6 43.6 %copy-start.1 = (f32[1,1,86,16]{3,2,1,0:T(8,128)S(1)}, f32[1,1,86,16]{3,2,1,0:T(8,128)}, u32[]{:S(2)}) copy-start(f32[1,1,86,16]{3,2,1,0:T(8,128)} %copy.42) | copy-start | bytes 16516
  186.0 62.8 %copy-start.6 = (f32[8,128]{1,0:T(8,128)}, f32[8,128]{1,0:T(8,128)S(1)}, u32[]{:S(2)}) copy-start(f32[8,128]{1,0:T(8,128)S(1)} %multiply_add_fusion) | copy-start | bytes 12292
Sparse Core Ops, SparseCore 0:
  16.9 19.1 all-gather.2
  188.2 57.5 all-gather.4
where the time goes:
time: 262 us; the launch traced here: 261 us
  waiting for transfers between devices  132 us (50%)
  blocking collectives  37.9 us (14%)
  other arithmetic  33 us (13%)
  local copies, waits for them, and re-layouts  25.3 us (10%)
  between operations  14.3 us (5%)
  starting transfers between devices  10.9 us (4%)
  matrix products  7.46 us (3%)
    all_to_all x1, waiting for transfers between devices, on_device(): lax.all_to_all(outgoing.astype(jnp.bfloat16), 'grp', split_axis=0, concat...  58.6 us
    all_gather x1, waiting for transfers between devices, on_device(): collected = lax.all_gather(updated, 'grp', axis=0, tiled=True)  56.8 us
    psum x1, blocking collectives, on_device(): col_total, row_total = lax.psum((col_part, row_part), ('grp', 'intra'))  37.9 us
    add x4, other arithmetic, add_term(): return (total + term.astype(jnp.float32), None)  18.6 us
    unnamed x20, local copies, waits for them, and re-layouts  10.5 us
    all_to_all x1, waiting for transfers between devices, on_device(): lax.all_to_all(scaled, 'intra', split_axis=1, concat_axis=0, tiled=True)  8.75 us
    all_gather x1, waiting for transfers between devices, on_device(): peer_grads = lax.all_gather(cotangent, 'intra', axis=0, tiled=True)  7.13 us
    all_to_all x1, starting transfers between devices, on_device(): lax.all_to_all(outgoing.astype(jnp.bfloat16), 'grp', split_axis=0, concat...  6.61 us
  transfers between devices with their start and end apart: 4, of which 4 were waited for; matrix products, arithmetic and copies ran while one was open for 4% of the time, Pallas kernels for 0%

commit v1 on v0

v1 whole, which is shorter than its diff:
```python
import functools

import jax
import jax.numpy as jnp
from jax import lax
from jax.experimental import pallas as pl
from jax.experimental.pallas import tpu as pltpu
from jax.sharding import PartitionSpec as P

decay_rate = 0.8
step_size = 0.5
epsilon = 1e-06

MESH = pl.DeviceIdType.MESH
HIGH = lax.Precision.HIGHEST
CHUNKS = 4


def to_units(block, blocks, unit_rows, tensors, head):
    return (
        block.reshape(blocks, unit_rows, tensors, head)
        .transpose(2, 0, 1, 3)
        .reshape(tensors * blocks, unit_rows * head)
    )


def from_units(units, blocks, unit_rows, tensors, head):
    return (
        units.reshape(tensors, blocks, unit_rows, head)
        .transpose(1, 2, 0, 3)
        .reshape(blocks * unit_rows, tensors * head)
    )


def pick(hot, rows):
    return jnp.dot(hot.astype(jnp.bfloat16), rows, preferred_element_type=jnp.float32)


def general(normed, cotangent, norm_gain, weights, row_state, col_state, owner_table):
    groups = lax.axis_size("grp")
    members = lax.axis_size("intra")
    d_model = normed.shape[1]
    tokens_here = cotangent.shape[0]
    width = cotangent.shape[1]
    tensors = col_state.shape[0]
    head = col_state.shape[1]
    capacity = row_state.shape[2]
    unit_rows = row_state.shape[3]
    slab_rows = weights.shape[0]
    blocks = slab_rows // unit_rows
    unit_count = tensors * blocks
    scaled = (normed * norm_gain[None, :]).astype(jnp.bfloat16)
    columns = lax.all_to_all(scaled, "intra", split_axis=1, concat_axis=0, tiled=True)
    peer_grads = lax.all_gather(cotangent, "intra", axis=0, tiled=True)

    def add_term(total, pair):
        left, right = pair
        term = lax.dot_general(
            left, right, (((0,), (0,)), ((), ())), preferred_element_type=jnp.float32
        )
        return (total + term, None)

    slab, _ = lax.scan(
        add_term,
        jnp.zeros((slab_rows, width), jnp.float32),
        (
            columns.reshape(members, tokens_here, slab_rows),
            peer_grads.reshape(members, tokens_here, width),
        ),
    )
    owner_flat = owner_table[:, 0]
    owner_hot = owner_flat[:, None] == jnp.arange(groups, dtype=jnp.int32)[None, :]
    ids = jnp.arange(unit_count, dtype=jnp.int32)
    earlier = (owner_flat[:, None] == owner_flat[None, :]) & (ids[None, :] < ids[:, None])
    slot = jnp.sum(earlier.astype(jnp.int32), axis=1)
    place = owner_flat * capacity + slot
    hot = place[:, None] == jnp.arange(groups * capacity, dtype=jnp.int32)[None, :]
    my_group = lax.axis_index("grp")
    my_place = my_group * capacity + jnp.arange(capacity, dtype=jnp.int32)
    my_hot = my_place[:, None] == place[None, :]
    valid = jnp.any(my_hot, axis=1)
    weight_units = to_units(weights, blocks, unit_rows, tensors, head)
    grad_units = to_units(slab, blocks, unit_rows, tensors, head).astype(jnp.bfloat16)
    outgoing = pick(hot.T, grad_units).reshape(groups, capacity, unit_rows, head)
    incoming = lax.all_to_all(
        outgoing.astype(jnp.bfloat16), "grp", split_axis=0, concat_axis=0, tiled=True
    ).astype(jnp.float32)
    grad_own = jnp.sum(incoming, axis=0)
    own_weights = pick(my_hot, weight_units).reshape(capacity, unit_rows, head)
    unit_hot = (
        (ids // blocks)[:, None] == jnp.arange(tensors, dtype=jnp.int32)[None, :]
    ).astype(jnp.bfloat16)
    tensor_hot = pick(my_hot, unit_hot)
    squares = grad_own * grad_own
    row_mean = jnp.mean(squares, axis=2) + epsilon
    row_new = jnp.where(
        valid[:, None], decay_rate * row_state[0, 0] + (1.0 - decay_rate) * row_mean, 0.0
    )
    col_part = jnp.einsum("st,srh->th", tensor_hot, squares, precision=HIGH)
    row_part = jnp.einsum("st,sr->t", tensor_hot, row_new, precision=HIGH)
    col_total, row_total = lax.psum((col_part, row_part), ("grp", "intra"))
    col_new = decay_rate * col_state + (1.0 - decay_rate) * (col_total / d_model + epsilon)
    row_avg = row_total / d_model
    col_slot = jnp.dot(tensor_hot, col_new, precision=HIGH)
    avg_slot = jnp.where(valid, jnp.dot(tensor_hot, row_avg, precision=HIGH), 1.0)
    variance = row_new[:, :, None] * col_slot[:, None, :] / avg_slot[:, None, None]
    variance = jnp.where(valid[:, None, None], variance, 1.0)
    updated = (own_weights - step_size * grad_own / jnp.sqrt(variance)).astype(jnp.bfloat16)
    collected = lax.all_gather(updated, "grp", axis=0, tiled=True)
    mine = pick(hot, collected.reshape(groups * capacity, unit_rows * head)).astype(jnp.bfloat16)
    new_weights = from_units(mine, blocks, unit_rows, tensors, head)
    return (new_weights, row_new[None, None], col_new)


def iota(shape, axis):
    return lax.broadcasted_iota(jnp.int32, shape, axis)


def kernel(
    d_model,
    normed,
    cot,
    gain,
    weights,
    state,
    col_state,
    owner,
    out,
    row_out,
    col_out,
    x_all,
    c_all,
    w_own,
    st_all,
    slots,
    owners,
    prev,
    part,
    x_recv,
    z_send,
    z_recv,
    grad,
    rows_new,
    stat,
    note,
    new_own,
    local_sem,
    cs,
    cr,
    xs,
    xr,
    ss,
    sr,
    ps,
    pr,
    zs,
    zr,
    ts,
    tr,
    ns,
    nr,
    us,
    ur,
    fs,
    fr,
):
    groups = lax.axis_size("grp")
    members = lax.axis_size("intra")
    g = lax.axis_index("grp")
    i = lax.axis_index("intra")
    z, x = g // 2, g % 2
    zn = groups // 2
    tokens = cot.shape[0]
    slab = grad.shape[0]
    head = grad.shape[1]
    capacity, unit_rows = state.shape[1], state.shape[0]
    units = owner.shape[1]
    blocks = slab // unit_rows
    step = slab // CHUNKS
    other_core = i // 2 * 2 + (1 - i % 2)
    other_y = (1 - i // 2) * 2 + i % 2
    other_x = z * 2 + (1 - x)

    def grp_peer(d):
        return lax.rem(g + d, groups)

    def z_peer(d):
        return lax.rem(z + d, zn) * 2 + x

    def intra_peer(d):
        return lax.rem(i + d, members)

    def remote(src, dst, send, recv, to):
        return pltpu.make_async_remote_copy(
            src_ref=src, dst_ref=dst, send_sem=send, recv_sem=recv, device_id=to, device_id_type=MESH
        )

    local = [
        pltpu.make_async_copy(cot, c_all.at[i], local_sem.at[0]),
        pltpu.make_async_copy(
            normed.at[:, pl.ds(pl.multiple_of(i * slab, slab), slab)], x_all.at[0], local_sem.at[1]
        ),
        pltpu.make_async_copy(
            weights.at[:, pl.ds(pl.multiple_of(g * head, head), head)], w_own, local_sem.at[2]
        ),
    ]
    for copy in local:
        copy.start()

    barrier = pltpu.get_barrier_semaphore()
    for d in range(1, groups):
        pl.semaphore_signal(barrier, inc=1, device_id=(grp_peer(d), i), device_id_type=MESH)
    for d in range(1, members):
        pl.semaphore_signal(barrier, inc=1, device_id=(g, intra_peer(d)), device_id_type=MESH)
    st_all[0] = jnp.zeros_like(st_all[0])
    st_all[0, :, :capacity] = state[...]
    pl.semaphore_wait(barrier, groups + members - 2)

    cot_y = remote(cot, c_all.at[i], cs.at[0], cr.at[0], (g, other_y))
    cot_core = remote(cot, c_all.at[i], cs.at[1], cr.at[1], (g, other_core))
    cot_on = remote(c_all.at[other_y], c_all.at[other_y], cs.at[2], cr.at[2], (g, other_core))
    cot_y.start()
    cot_core.start()
    x_copies = {}
    for k in range(CHUNKS):
        for d in range(1, members):
            to = intra_peer(d)
            x_copies[k, d] = remote(
                normed.at[:, pl.ds(pl.multiple_of(to * slab + k * step, step), step)],
                x_all.at[d, :, pl.ds(k * step, step)],
                xs.at[k, d],
                xr.at[k, d],
                (g, to),
            )
            x_copies[k, d].start()
    state_copies = []
    for d in range(1, groups):
        copy = remote(st_all.at[0], st_all.at[d], ss.at[d], sr.at[d], (grp_peer(d), i))
        copy.start()
        state_copies.append(copy)

    own_row = owner[...]
    mine_col = jnp.sum(
        jnp.where(iota((units, units), 0) == iota((units, units), 1), own_row, 0).astype(jnp.float32),
        axis=1,
        keepdims=True,
    )
    same = (mine_col == own_row.astype(jnp.float32)) & (iota((units, units), 1) < iota((units, units), 0))
    slots[...] = jnp.sum(jnp.where(same, 1.0, 0.0), axis=1, keepdims=True)
    owners[...] = mine_col

    cot_y.wait_recv()
    cot_on.start()
    for copy in state_copies:
        copy.wait_recv()
    base = pl.ds(pl.multiple_of(g * blocks, blocks), blocks)
    my_owner, my_slot = owners[base, :], slots[base, :]
    lane = iota((blocks, 128), 1).astype(jnp.float32)
    old = jnp.zeros((blocks, unit_rows), jnp.float32)
    for d in range(groups):
        source = lax.rem(g + groups - d, groups).astype(jnp.float32)
        hot = jnp.where((lane == my_slot) & (my_owner == source), 1.0, 0.0)
        old = old + lax.dot_general(
            hot, st_all[d], (((1,), (1,)), ((), ())), precision=HIGH, preferred_element_type=jnp.float32
        )

    def expand():
        return jnp.where(iota((slab, blocks), 0) // unit_rows == iota((slab, blocks), 1), 1.0, 0.0)

    def diagonal():
        return iota((slab, unit_rows), 0) % unit_rows == iota((slab, unit_rows), 1)

    spread = lax.dot_general(
        expand(), old, (((1,), (0,)), ((), ())), precision=HIGH, preferred_element_type=jnp.float32
    )
    prev[...] = jnp.sum(jnp.where(diagonal(), spread, 0.0), axis=1, keepdims=True)

    for copy in local:
        copy.wait()
    cot_core.wait_recv()
    cot_on.wait_recv()

    def rows(k):
        return pl.ds(k * step, step)

    part_copies, z_copies = {}, {}

    def multiply(k):
        for d in range(1, members):
            x_copies[k, d].wait_recv()
        gains = gain[:, pl.ds(pl.multiple_of(i * slab + k * step, step), step)]
        total = jnp.zeros((step, cot.shape[1]), jnp.float32)
        for d in range(members):
            scaled = (x_all[d, :, rows(k)].astype(jnp.float32) * gains).astype(jnp.bfloat16)
            total = total + lax.dot_general(
                scaled,
                c_all[lax.rem(i + members - d, members)],
                (((0,), (0,)), ((), ())),
                preferred_element_type=jnp.float32,
            )
        total = total.astype(jnp.bfloat16)
        for t in range(groups):
            part[t // 2, t % 2, rows(k), :] = total[:, t * head : (t + 1) * head]
        part_copies[k] = remote(
            part.at[:, 1 - x, rows(k), :], x_recv.at[:, rows(k), :], ps.at[k], pr.at[k], (other_x, i)
        )
        part_copies[k].start()

    def pass_on(k):
        part_copies[k].wait_recv()
        for d in range(zn):
            to = lax.rem(z + d, zn)
            both = part[to, x, rows(k), :].astype(jnp.float32) + x_recv[to, rows(k), :].astype(jnp.float32)
            if d == 0:
                grad[rows(k), :] = both
                continue
            z_send[d, rows(k), :] = both.astype(jnp.bfloat16)
            z_copies[k, d] = remote(
                z_send.at[d, rows(k), :], z_recv.at[d, rows(k), :], zs.at[k, d], zr.at[k, d], (z_peer(d), i)
            )
            z_copies[k, d].start()

    sums = []

    def finish(k):
        total = grad[rows(k), :]
        for d in range(1, zn):
            z_copies[k, d].wait_recv()
            total = total + z_recv[d, rows(k), :].astype(jnp.float32)
        grad[rows(k), :] = total
        squares = total * total
        mean = jnp.sum(squares, axis=1, keepdims=True) / head + epsilon
        row = decay_rate * prev[rows(k), :] + (1.0 - decay_rate) * mean
        rows_new[rows(k), :] = row
        sums.append(
            (jnp.sum(squares, axis=0, keepdims=True), jnp.sum(jnp.broadcast_to(row, squares.shape), axis=0, keepdims=True))
        )

    for k in range(CHUNKS + 2):
        if k < CHUNKS:
            multiply(k)
        if 0 <= k - 1 < CHUNKS:
            pass_on(k - 1)
        if 0 <= k - 2:
            finish(k - 2)

    stat[0, 0:1, :] = sum(s[0] for s in sums)
    stat[0, 1:2, :] = sum(s[1] for s in sums)
    stat_copies = []
    for d in range(1, members):
        copy = remote(stat.at[0], stat.at[d], ts.at[d], tr.at[d], (g, intra_peer(d)))
        copy.start()
        stat_copies.append(copy)
    note[0, 0:unit_rows, 0:blocks] = lax.dot_general(
        jnp.where(diagonal(), rows_new[...], 0.0),
        expand(),
        (((0,), (0,)), ((), ())),
        precision=HIGH,
        preferred_element_type=jnp.float32,
    )
    for copy in stat_copies:
        copy.wait_recv()
    col_total = stat[0, 0:1, :]
    row_total = stat[0, 1:2, :]
    for d in range(1, members):
        col_total = col_total + stat[d, 0:1, :]
        row_total = row_total + stat[d, 1:2, :]
    col_new = decay_rate * col_state[pl.ds(g, 1), :] + (1.0 - decay_rate) * (col_total / d_model + epsilon)
    note[0, unit_rows : unit_rows + 1, :] = col_new
    col_factor = step_size * lax.rsqrt(col_new / (row_total / d_model))

    note_copies = []
    for d in range(1, groups):
        copy = remote(note.at[0], note.at[d], ns.at[d], nr.at[d], (grp_peer(d), i))
        copy.start()
        note_copies.append(copy)

    def columns(t):
        return pl.ds(pl.multiple_of(t * head, head), head)

    new_copies, forwards = {}, {}
    for k in range(CHUNKS):
        change = grad[rows(k), :] * lax.rsqrt(rows_new[rows(k), :]) * col_factor
        fresh = (w_own[rows(k), :].astype(jnp.float32) - change).astype(jnp.bfloat16)
        new_own[rows(k), :] = fresh
        out[rows(k), columns(g)] = fresh
        for d in range(1, zn):
            new_copies[k, d] = remote(
                new_own.at[rows(k), :], out.at[rows(k), columns(g)], us.at[k, d], ur.at[k, d], (z_peer(d), i)
            )
            new_copies[k, d].start()
        forwards[k, 0] = remote(
            new_own.at[rows(k), :], out.at[rows(k), columns(g)], fs.at[k, 0], fr.at[k, 0], (other_x, i)
        )
        forwards[k, 0].start()
    for k in range(CHUNKS):
        for d in range(1, zn):
            new_copies[k, d].wait_recv()
            at = columns(lax.rem(z + zn - d, zn) * 2 + x)
            forwards[k, d] = remote(
                out.at[rows(k), at], out.at[rows(k), at], fs.at[k, d], fr.at[k, d], (other_x, i)
            )
            forwards[k, d].start()

    for copy in note_copies:
        copy.wait_recv()
    got = jnp.zeros((unit_rows, 128), jnp.float32)
    me = g.astype(jnp.float32)
    for d in range(groups):
        t = lax.rem(g + groups - d, groups)
        at = pl.ds(pl.multiple_of(t * blocks, blocks), blocks)
        hot = jnp.where((lane == slots[at, :]) & (owners[at, :] == me), 1.0, 0.0)
        got = got + lax.dot_general(
            note[d, 0:unit_rows, 0:blocks],
            hot,
            (((1,), (0,)), ((), ())),
            precision=HIGH,
            preferred_element_type=jnp.float32,
        )
        col_out[pl.ds(t, 1), :] = note[d, unit_rows : unit_rows + 1, :]
    row_out[...] = got[:, :capacity]

    for k in range(CHUNKS):
        for d in range(zn):
            forwards[k, d].wait_recv()
    sent = [cot_y, cot_core, cot_on, *x_copies.values(), *state_copies, *part_copies.values()]
    sent += [*z_copies.values(), *stat_copies, *note_copies, *new_copies.values(), *forwards.values()]
    for copy in sent:
        copy.wait_send()


def fused(normed, cotangent, norm_gain, weights, row_state, col_state, owner_table):
    groups = lax.axis_size("grp")
    members = lax.axis_size("intra")
    tokens, d_model = normed.shape
    slab, width = weights.shape
    tensors, head = col_state.shape
    capacity, unit_rows = row_state.shape[2:]
    units = owner_table.shape[0]
    zn = groups // 2
    bf16, f32 = jnp.bfloat16, jnp.float32
    vmem = pl.BlockSpec(memory_space=pltpu.VMEM)
    anywhere = pl.BlockSpec(memory_space=pl.ANY)
    dma = pltpu.SemaphoreType.DMA
    note_rows = unit_rows + 8
    out, row_out, col_out = pl.pallas_call(
        functools.partial(kernel, d_model),
        out_shape=(
            jax.ShapeDtypeStruct((slab, width), bf16),
            jax.ShapeDtypeStruct((unit_rows, capacity), f32),
            jax.ShapeDtypeStruct((tensors, head), f32),
        ),
        in_specs=[anywhere, anywhere, vmem, anywhere, vmem, vmem, vmem],
        out_specs=(vmem, vmem, vmem),
        scratch_shapes=[
            pltpu.VMEM((members, tokens, slab), bf16),
            pltpu.VMEM((members, tokens, width), bf16),
            pltpu.VMEM((slab, head), bf16),
            pltpu.VMEM((groups, unit_rows, 128), f32),
            pltpu.VMEM((units, 1), f32),
            pltpu.VMEM((units, 1), f32),
            pltpu.VMEM((slab, 1), f32),
            pltpu.VMEM((zn, 2, slab, head), bf16),
            pltpu.VMEM((zn, slab, head), bf16),
            pltpu.VMEM((zn, slab, head), bf16),
            pltpu.VMEM((zn, slab, head), bf16),
            pltpu.VMEM((slab, head), f32),
            pltpu.VMEM((slab, 1), f32),
            pltpu.VMEM((members, 8, head), f32),
            pltpu.VMEM((groups, note_rows, 128), f32),
            pltpu.VMEM((slab, head), bf16),
            dma((3,)),
            dma((3,)),
            dma((3,)),
            dma((CHUNKS, members)),
            dma((CHUNKS, members)),
            dma((groups,)),
            dma((groups,)),
            dma((CHUNKS,)),
            dma((CHUNKS,)),
            dma((CHUNKS, zn)),
            dma((CHUNKS, zn)),
            dma((members,)),
            dma((members,)),
            dma((groups,)),
            dma((groups,)),
            dma((CHUNKS, zn)),
            dma((CHUNKS, zn)),
            dma((CHUNKS, zn)),
            dma((CHUNKS, zn)),
        ],
        compiler_params=pltpu.CompilerParams(
            collective_id=0, has_side_effects=True, vmem_limit_bytes=40 * 2**20
        ),
        cost_estimate=pl.CostEstimate(
            flops=2 * members * tokens * slab * width, bytes_accessed=6 * 2**20, transcendentals=0
        ),
    )(
        normed,
        cotangent,
        norm_gain.reshape(1, d_model),
        weights,
        row_state[0, 0].T,
        col_state,
        owner_table.reshape(1, units),
    )
    return (out, row_out.T[None, None], col_out)


def solution(mesh):
    placed = (
        P(("grp", "intra"), None),
        P(("grp", "intra"), None),
        P(),
        P("intra", None),
        P("grp", "intra", None, None),
        P(),
        P(),
    )
    fits = mesh.shape["grp"] == 8 and mesh.shape["intra"] == 4
    return jax.shard_map(
        fused if fits else general,
        mesh=mesh,
        in_specs=placed,
        out_specs=(P("intra", None), P("grp", "intra", None, None), P()),
        check_vma=False,
    )
```

time: 262 us -> 94.7 us (0.36)
  the two profiles are of different devices: /device:TPU:0 before, /device:TPU:24 now
where the time goes in v1:
time: 94.7 us; the launch traced here: 94.4 us
  Pallas kernels  84.7 us (89%)
  local copies, waits for them, and re-layouts  9.05 us (10%)
    pallas_call x1, Pallas kernels, fused(): pl.pallas_call(functools.partial(kernel, d_model), out_shape=(jax.ShapeDt...  84.7 us
    unnamed x17, local copies, waits for them, and re-layouts  9.05 us

profile of v1, /device:TPU:24, one launch (start us, length us, event | category | flops | bytes accessed | tf_op | source)
XLA Modules:
  0.0 94.4 jit_solution(3824924251322273178)
XLA Ops:
  0.6 0.0 copy-start
  0.6 1.6 %copy-done = bf16[1024,1024]{1,0:T(8,128)(2,1)S(1)} copy-done((bf16[1024,1024]{1,0:T(8,128)(2,1)S(1)}, bf16[1024,1024]{1,0:T(8,128)(2,1)}, u32[]{:S(2)}) %copy-start) | copy-done | bytes 2097176
  2.2 0.0 copy-start.1
  2.2 1.2 %copy-done.1 = bf16[128,4096]{1,0:T(8,128)(2,1)S(1)} copy-done((bf16[128,4096]{1,0:T(8,128)(2,1)S(1)}, bf16[128,4096]{1,0:T(8,128)(2,1)}, u32[]{:S(2)}) %copy-start.1) | copy-done | bytes 1048600
  3.5 0.0 copy-start.2
  3.5 0.9 %copy-done.2 = bf16[128,1024]{1,0:T(8,128)(2,1)S(1)} copy-done((bf16[128,1024]{1,0:T(8,128)(2,1)S(1)}, bf16[128,1024]{1,0:T(8,128)(2,1)}, u32[]{:S(2)}) %copy-start.2) | copy-done | bytes 262168
  4.4 0.0 copy-start.3
  4.4 0.7 copy-done.3
  5.1 0.0 copy-start.4
  5.1 0.7 copy-done.4
  5.8 0.0 copy-start.5
  5.8 0.7 copy-done.5
  6.5 0.0 copy-start.6
  6.5 0.7 copy-done.6
  7.2 84.7 %shard_map.94 = (bf16[1024,1024]{1,0:T(8,128)(2,1)S(1)}, f32[16,86]{1,0:T(8,128)S(1)}, f32[8,128]{1,0:T(8,128)S(1)}) custom-call(bf16[128,4096]{1,0:T(8,128)(2,1)S(1)} %copy-done.1, bf16[128,1024]{1,0:T(8,128)(2,1)S(1)} %copy-done.2, f32[1,4096]{1,0:T(1,128)S(1)} %bitcast.9, bf16[1024,1024]{1,0:T(8,128)(2,1)S(1)} %copy-done, f32[16,86]{1,0:T(8,128)S(1)} %bitcast.10, ...), custom_call_target="tpu_custom_call" | custom-call | flops 1073741824 | bytes 6291456 | tf_op jit(solution)/shard_map/pallas_call | solution.py:446
  91.9 1.3 %copy.13 = bf16[1024,1024]{1,0:T(8,128)(2,1)} copy(bf16[1024,1024]{1,0:T(8,128)(2,1)S(1)} %get-tuple-element.12) | data formatting | bytes 4194304
  93.2 0.6 copy.14
  93.8 0.6 copy.15
Async XLA Ops:
  0.6 1.6 %copy-start = (bf16[1024,1024]{1,0:T(8,128)(2,1)S(1)}, bf16[1024,1024]{1,0:T(8,128)(2,1)}, u32[]{:S(2)}) copy-start(bf16[1024,1024]{1,0:T(8,128)(2,1)} %weights.1) | copy-start | bytes 6291460
  2.2 1.2 %copy-start.1 = (bf16[128,4096]{1,0:T(8,128)(2,1)S(1)}, bf16[128,4096]{1,0:T(8,128)(2,1)}, u32[]{:S(2)}) copy-start(bf16[128,4096]{1,0:T(8,128)(2,1)} %normed.1) | copy-start | bytes 3145732
  3.5 0.9 %copy-start.2 = (bf16[128,1024]{1,0:T(8,128)(2,1)S(1)}, bf16[128,1024]{1,0:T(8,128)(2,1)}, u32[]{:S(2)}) copy-start(bf16[128,1024]{1,0:T(8,128)(2,1)} %cot.1) | copy-start | bytes 786436
  4.4 0.7 copy-start.3
  5.1 0.7 copy-start.4
  5.8 0.7 copy-start.5
  6.5 0.7 copy-start.6

commit v2 on v1

--- a/solution.py
+++ b/solution.py
@@ -13,7 +13,7 @@
 
 MESH = pl.DeviceIdType.MESH
 HIGH = lax.Precision.HIGHEST
-CHUNKS = 4
+CHUNKS = 8
 
 
 def to_units(block, blocks, unit_rows, tensors, head):
@@ -120,30 +120,35 @@
     d_model,
     normed,
     cot,
+    gain_in,
+    weights,
+    state_in,
+    col_in,
+    owner_in,
+    out,
+    row_out,
+    col_out,
     gain,
-    weights,
     state,
     col_state,
     owner,
-    out,
-    row_out,
-    col_out,
     x_all,
     c_all,
-    w_own,
+    w_all,
     st_all,
     slots,
     owners,
-    prev,
+    old,
+    factor,
     part,
     x_recv,
     z_send,
     z_recv,
     grad,
     rows_new,
+    gathered,
     stat,
     note,
-    new_own,
     local_sem,
     cs,
     cr,
@@ -170,7 +175,6 @@
     i = lax.axis_index("intra")
     z, x = g // 2, g % 2
     zn = groups // 2
-    tokens = cot.shape[0]
     slab = grad.shape[0]
     head = grad.shape[1]
     capacity, unit_rows = state.shape[1], state.shape[0]
@@ -195,25 +199,27 @@
             src_ref=src, dst_ref=dst, send_sem=send, recv_sem=recv, device_id=to, device_id_type=MESH
         )
 
-    local = [
-        pltpu.make_async_copy(cot, c_all.at[i], local_sem.at[0]),
-        pltpu.make_async_copy(
-            normed.at[:, pl.ds(pl.multiple_of(i * slab, slab), slab)], x_all.at[0], local_sem.at[1]
-        ),
-        pltpu.make_async_copy(
-            weights.at[:, pl.ds(pl.multiple_of(g * head, head), head)], w_own, local_sem.at[2]
-        ),
-    ]
-    for copy in local:
-        copy.start()
-
     barrier = pltpu.get_barrier_semaphore()
     for d in range(1, groups):
         pl.semaphore_signal(barrier, inc=1, device_id=(grp_peer(d), i), device_id_type=MESH)
     for d in range(1, members):
         pl.semaphore_signal(barrier, inc=1, device_id=(g, intra_peer(d)), device_id_type=MESH)
-    st_all[0] = jnp.zeros_like(st_all[0])
-    st_all[0, :, :capacity] = state[...]
+
+    slab_at = pl.ds(pl.multiple_of(i * slab, slab), slab)
+    local = [
+        pltpu.make_async_copy(state_in, state, local_sem.at[0]),
+        pltpu.make_async_copy(owner_in, owner, local_sem.at[1]),
+        pltpu.make_async_copy(cot, c_all.at[i], local_sem.at[2]),
+        pltpu.make_async_copy(normed.at[:, slab_at], x_all.at[0], local_sem.at[3]),
+        pltpu.make_async_copy(gain_in.at[:, slab_at], gain, local_sem.at[4]),
+        pltpu.make_async_copy(col_in, col_state, local_sem.at[5]),
+        pltpu.make_async_copy(weights, w_all, local_sem.at[6]),
+    ]
+    for copy in local:
+        copy.start()
+    st_all[g] = jnp.zeros_like(st_all[0])
+    local[0].wait()
+    st_all[g, :, :capacity] = state[...]
     pl.semaphore_wait(barrier, groups + members - 2)
 
     cot_y = remote(cot, c_all.at[i], cs.at[0], cr.at[0], (g, other_y))
@@ -235,17 +241,16 @@
             x_copies[k, d].start()
     state_copies = []
     for d in range(1, groups):
-        copy = remote(st_all.at[0], st_all.at[d], ss.at[d], sr.at[d], (grp_peer(d), i))
+        copy = remote(st_all.at[g], st_all.at[g], ss.at[d], sr.at[d], (grp_peer(d), i))
         copy.start()
         state_copies.append(copy)
 
-    own_row = owner[...]
+    local[1].wait()
+    own_row = owner[...].astype(jnp.float32)
     mine_col = jnp.sum(
-        jnp.where(iota((units, units), 0) == iota((units, units), 1), own_row, 0).astype(jnp.float32),
-        axis=1,
-        keepdims=True,
-    )
-    same = (mine_col == own_row.astype(jnp.float32)) & (iota((units, units), 1) < iota((units, units), 0))
+        jnp.where(iota((units, units), 0) == iota((units, units), 1), own_row, 0.0), axis=1, keepdims=True
+    )
+    same = (mine_col == own_row) & (iota((units, units), 1) < iota((units, units), 0))
     slots[...] = jnp.sum(jnp.where(same, 1.0, 0.0), axis=1, keepdims=True)
     owners[...] = mine_col
 
@@ -253,16 +258,14 @@
     cot_on.start()
     for copy in state_copies:
         copy.wait_recv()
-    base = pl.ds(pl.multiple_of(g * blocks, blocks), blocks)
-    my_owner, my_slot = owners[base, :], slots[base, :]
-    lane = iota((blocks, 128), 1).astype(jnp.float32)
-    old = jnp.zeros((blocks, unit_rows), jnp.float32)
-    for d in range(groups):
-        source = lax.rem(g + groups - d, groups).astype(jnp.float32)
-        hot = jnp.where((lane == my_slot) & (my_owner == source), 1.0, 0.0)
-        old = old + lax.dot_general(
-            hot, st_all[d], (((1,), (1,)), ((), ())), precision=HIGH, preferred_element_type=jnp.float32
-        )
+    lane = iota((units, 128), 1).astype(jnp.float32)
+    total_old = jnp.zeros((units, unit_rows), jnp.float32)
+    for o in range(groups):
+        hot = jnp.where((lane == slots[...]) & (owners[...] == o), 1.0, 0.0)
+        total_old = total_old + lax.dot_general(
+            hot, st_all[o], (((1,), (1,)), ((), ())), precision=HIGH, preferred_element_type=jnp.float32
+        )
+    old[...] = total_old
 
     def expand():
         return jnp.where(iota((slab, blocks), 0) // unit_rows == iota((slab, blocks), 1), 1.0, 0.0)
@@ -270,12 +273,19 @@
     def diagonal():
         return iota((slab, unit_rows), 0) % unit_rows == iota((slab, unit_rows), 1)
 
-    spread = lax.dot_general(
-        expand(), old, (((1,), (0,)), ((), ())), precision=HIGH, preferred_element_type=jnp.float32
-    )
-    prev[...] = jnp.sum(jnp.where(diagonal(), spread, 0.0), axis=1, keepdims=True)
-
-    for copy in local:
+    def spread(t):
+        wide = lax.dot_general(
+            expand(),
+            old[t * blocks : (t + 1) * blocks, :],
+            (((1,), (0,)), ((), ())),
+            precision=HIGH,
+            preferred_element_type=jnp.float32,
+        )
+        factor[t] = jnp.sum(jnp.where(diagonal(), wide, 0.0), axis=1, keepdims=True)
+
+    for t in range(groups // 2):
+        spread(t)
+    for copy in local[2:]:
         copy.wait()
     cot_core.wait_recv()
     cot_on.wait_recv()
@@ -283,12 +293,18 @@
     def rows(k):
         return pl.ds(k * step, step)
 
-    part_copies, z_copies = {}, {}
+    def row_moments(t, k, squares):
+        mean = jnp.sum(squares, axis=1, keepdims=True) / head + epsilon
+        row = decay_rate * factor[t, rows(k), :] + (1.0 - decay_rate) * mean
+        factor[t, rows(k), :] = lax.rsqrt(row)
+        return row
+
+    part_copies, z_copies, own_copies, forwards = {}, {}, {}, {}
 
     def multiply(k):
         for d in range(1, members):
             x_copies[k, d].wait_recv()
-        gains = gain[:, pl.ds(pl.multiple_of(i * slab + k * step, step), step)]
+        gains = gain[:, rows(k)]
         total = jnp.zeros((step, cot.shape[1]), jnp.float32)
         for d in range(members):
             scaled = (x_all[d, :, rows(k)].astype(jnp.float32) * gains).astype(jnp.bfloat16)
@@ -308,10 +324,10 @@
 
     def pass_on(k):
         part_copies[k].wait_recv()
-        for d in range(zn):
+        for d in range(1, zn + 1):
             to = lax.rem(z + d, zn)
             both = part[to, x, rows(k), :].astype(jnp.float32) + x_recv[to, rows(k), :].astype(jnp.float32)
-            if d == 0:
+            if d == zn:
                 grad[rows(k), :] = both
                 continue
             z_send[d, rows(k), :] = both.astype(jnp.bfloat16)
@@ -327,104 +343,114 @@
         for d in range(1, zn):
             z_copies[k, d].wait_recv()
             total = total + z_recv[d, rows(k), :].astype(jnp.float32)
-        grad[rows(k), :] = total
-        squares = total * total
-        mean = jnp.sum(squares, axis=1, keepdims=True) / head + epsilon
-        row = decay_rate * prev[rows(k), :] + (1.0 - decay_rate) * mean
+        total = total.astype(jnp.bfloat16)
+        gathered[g, rows(k), :] = total
+        mine = gathered.at[g, rows(k), :]
+        for d in range(1, zn):
+            own_copies[k, d] = remote(mine, mine, us.at[k, d], ur.at[k, d], (z_peer(d), i))
+            own_copies[k, d].start()
+        forwards[k, 0] = remote(mine, mine, fs.at[k, 0], fr.at[k, 0], (other_x, i))
+        forwards[k, 0].start()
+        squares = total.astype(jnp.float32) * total.astype(jnp.float32)
+        row = row_moments(g, k, squares)
         rows_new[rows(k), :] = row
         sums.append(
             (jnp.sum(squares, axis=0, keepdims=True), jnp.sum(jnp.broadcast_to(row, squares.shape), axis=0, keepdims=True))
         )
 
-    for k in range(CHUNKS + 2):
+    def absorb(t, k):
+        value = gathered[t, rows(k), :].astype(jnp.float32)
+        row_moments(t, k, value * value)
+
+    def forward(k):
+        for d in range(1, zn):
+            t = lax.rem(z + zn - d, zn) * 2 + x
+            own_copies[k, d].wait_recv()
+            block = gathered.at[t, rows(k), :]
+            forwards[k, d] = remote(block, block, fs.at[k, d], fr.at[k, d], (other_x, i))
+            forwards[k, d].start()
+        for d in range(1, zn):
+            absorb(lax.rem(z + zn - d, zn) * 2 + x, k)
+
+    def arrive(k):
+        for d in range(zn):
+            forwards[k, d].wait_recv()
+            absorb(lax.rem(z + zn - d, zn) * 2 + 1 - x, k)
+
+    stat_copies, note_copies = [], []
+
+    def share_sums():
+        stat[i, 0:1, :] = sum(s[0] for s in sums)
+        stat[i, 1:2, :] = sum(s[1] for s in sums)
+        for d in range(1, members):
+            copy = remote(stat.at[i], stat.at[i], ts.at[d], tr.at[d], (g, intra_peer(d)))
+            copy.start()
+            stat_copies.append(copy)
+        note[g, 0:unit_rows, 0:blocks] = lax.dot_general(
+            jnp.where(diagonal(), rows_new[...], 0.0),
+            expand(),
+            (((0,), (0,)), ((), ())),
+            precision=HIGH,
+            preferred_element_type=jnp.float32,
+        )
+
+    def share_note():
+        for copy in stat_copies:
+            copy.wait_recv()
+        col_total, row_total = stat[0, 0:1, :], stat[0, 1:2, :]
+        for m in range(1, members):
+            col_total = col_total + stat[m, 0:1, :]
+            row_total = row_total + stat[m, 1:2, :]
+        col_new = decay_rate * col_state[pl.ds(g, 1), :] + (1.0 - decay_rate) * (col_total / d_model + epsilon)
+        note[g, unit_rows : unit_rows + 1, :] = col_new
+        note[g, unit_rows + 1 : unit_rows + 2, :] = step_size * lax.rsqrt(col_new / (row_total / d_model))
+        for d in range(1, groups):
+            copy = remote(note.at[g], note.at[g], ns.at[d], nr.at[d], (grp_peer(d), i))
+            copy.start()
+            note_copies.append(copy)
+
+    for k in range(CHUNKS + 4):
         if k < CHUNKS:
             multiply(k)
+        if k < 2:
+            spread(groups // 2 + 2 * k)
+            spread(groups // 2 + 2 * k + 1)
         if 0 <= k - 1 < CHUNKS:
             pass_on(k - 1)
-        if 0 <= k - 2:
+        if 0 <= k - 2 < CHUNKS:
             finish(k - 2)
-
-    stat[0, 0:1, :] = sum(s[0] for s in sums)
-    stat[0, 1:2, :] = sum(s[1] for s in sums)
-    stat_copies = []
-    for d in range(1, members):
-        copy = remote(stat.at[0], stat.at[d], ts.at[d], tr.at[d], (g, intra_peer(d)))
-        copy.start()
-        stat_copies.append(copy)
-    note[0, 0:unit_rows, 0:blocks] = lax.dot_general(
-        jnp.where(diagonal(), rows_new[...], 0.0),
-        expand(),
-        (((0,), (0,)), ((), ())),
-        precision=HIGH,
-        preferred_element_type=jnp.float32,
-    )
-    for copy in stat_copies:
-        copy.wait_recv()
-    col_total = stat[0, 0:1, :]
-    row_total = stat[0, 1:2, :]
-    for d in range(1, members):
-        col_total = col_total + stat[d, 0:1, :]
-        row_total = row_total + stat[d, 1:2, :]
-    col_new = decay_rate * col_state[pl.ds(g, 1), :] + (1.0 - decay_rate) * (col_total / d_model + epsilon)
-    note[0, unit_rows : unit_rows + 1, :] = col_new
-    col_factor = step_size * lax.rsqrt(col_new / (row_total / d_model))
-
-    note_copies = []
-    for d in range(1, groups):
-        copy = remote(note.at[0], note.at[d], ns.at[d], nr.at[d], (grp_peer(d), i))
-        copy.start()
-        note_copies.append(copy)
-
-    def columns(t):
-        return pl.ds(pl.multiple_of(t * head, head), head)
-
-    new_copies, forwards = {}, {}
-    for k in range(CHUNKS):
-        change = grad[rows(k), :] * lax.rsqrt(rows_new[rows(k), :]) * col_factor
-        fresh = (w_own[rows(k), :].astype(jnp.float32) - change).astype(jnp.bfloat16)
-        new_own[rows(k), :] = fresh
-        out[rows(k), columns(g)] = fresh
-        for d in range(1, zn):
-            new_copies[k, d] = remote(
-                new_own.at[rows(k), :], out.at[rows(k), columns(g)], us.at[k, d], ur.at[k, d], (z_peer(d), i)
-            )
-            new_copies[k, d].start()
-        forwards[k, 0] = remote(
-            new_own.at[rows(k), :], out.at[rows(k), columns(g)], fs.at[k, 0], fr.at[k, 0], (other_x, i)
-        )
-        forwards[k, 0].start()
-    for k in range(CHUNKS):
-        for d in range(1, zn):
-            new_copies[k, d].wait_recv()
-            at = columns(lax.rem(z + zn - d, zn) * 2 + x)
-            forwards[k, d] = remote(
-                out.at[rows(k), at], out.at[rows(k), at], fs.at[k, d], fr.at[k, d], (other_x, i)
-            )
-            forwards[k, d].start()
+            if k - 2 == CHUNKS - 1:
+                share_sums()
+        if 0 <= k - 3 < CHUNKS:
+            forward(k - 3)
+            if k - 3 == CHUNKS - 1:
+                share_note()
+        if 0 <= k - 4 < CHUNKS:
+            arrive(k - 4)
 
     for copy in note_copies:
         copy.wait_recv()
+    for t in range(groups):
+        col_factor = note[t, unit_rows + 1 : unit_rows + 2, :]
+        at = slice(t * head, (t + 1) * head)
+        change = gathered[t].astype(jnp.float32) * factor[t] * col_factor
+        out[:, at] = (w_all[:, at].astype(jnp.float32) - change).astype(jnp.bfloat16)
+
     got = jnp.zeros((unit_rows, 128), jnp.float32)
-    me = g.astype(jnp.float32)
-    for d in range(groups):
-        t = lax.rem(g + groups - d, groups)
-        at = pl.ds(pl.multiple_of(t * blocks, blocks), blocks)
-        hot = jnp.where((lane == slots[at, :]) & (owners[at, :] == me), 1.0, 0.0)
+    hot = jnp.where((lane == slots[...]) & (owners[...] == g.astype(jnp.float32)), 1.0, 0.0)
+    for t in range(groups):
         got = got + lax.dot_general(
-            note[d, 0:unit_rows, 0:blocks],
-            hot,
+            note[t, 0:unit_rows, 0:blocks],
+            hot[t * blocks : (t + 1) * blocks],
             (((1,), (0,)), ((), ())),
             precision=HIGH,
             preferred_element_type=jnp.float32,
         )
-        col_out[pl.ds(t, 1), :] = note[d, unit_rows : unit_rows + 1, :]
+        col_out[t : t + 1, :] = note[t, unit_rows : unit_rows + 1, :]
     row_out[...] = got[:, :capacity]
 
-    for k in range(CHUNKS):
-        for d in range(zn):
-            forwards[k, d].wait_recv()
     sent = [cot_y, cot_core, cot_on, *x_copies.values(), *state_copies, *part_copies.values()]
-    sent += [*z_copies.values(), *stat_copies, *note_copies, *new_copies.values(), *forwards.values()]
+    sent += [*z_copies.values(), *stat_copies, *note_copies, *own_copies.values(), *forwards.values()]
     for copy in sent:
         copy.wait_send()
 
@@ -440,7 +466,7 @@
     zn = groups // 2
     bf16, f32 = jnp.bfloat16, jnp.float32
     vmem = pl.BlockSpec(memory_space=pltpu.VMEM)
-    anywhere = pl.BlockSpec(memory_space=pl.ANY)
+    hbm = pl.BlockSpec(memory_space=pltpu.HBM)
     dma = pltpu.SemaphoreType.DMA
     note_rows = unit_rows + 8
     out, row_out, col_out = pl.pallas_call(
@@ -450,26 +476,31 @@
             jax.ShapeDtypeStruct((unit_rows, capacity), f32),
             jax.ShapeDtypeStruct((tensors, head), f32),
         ),
-        in_specs=[anywhere, anywhere, vmem, anywhere, vmem, vmem, vmem],
+        in_specs=[hbm] * 7,
         out_specs=(vmem, vmem, vmem),
         scratch_shapes=[
+            pltpu.VMEM((1, slab), f32),
+            pltpu.VMEM((unit_rows, capacity), f32),
+            pltpu.VMEM((tensors, head), f32),
+            pltpu.VMEM((1, units), jnp.int32),
             pltpu.VMEM((members, tokens, slab), bf16),
             pltpu.VMEM((members, tokens, width), bf16),
-            pltpu.VMEM((slab, head), bf16),
+            pltpu.VMEM((slab, width), bf16),
             pltpu.VMEM((groups, unit_rows, 128), f32),
             pltpu.VMEM((units, 1), f32),
             pltpu.VMEM((units, 1), f32),
-            pltpu.VMEM((slab, 1), f32),
+            pltpu.VMEM((units, unit_rows), f32),
+            pltpu.VMEM((tensors, slab, 1), f32),
             pltpu.VMEM((zn, 2, slab, head), bf16),
             pltpu.VMEM((zn, slab, head), bf16),
             pltpu.VMEM((zn, slab, head), bf16),
             pltpu.VMEM((zn, slab, head), bf16),
             pltpu.VMEM((slab, head), f32),
             pltpu.VMEM((slab, 1), f32),
+            pltpu.VMEM((tensors, slab, head), bf16),
             pltpu.VMEM((members, 8, head), f32),
             pltpu.VMEM((groups, note_rows, 128), f32),
-            pltpu.VMEM((slab, head), bf16),
-            dma((3,)),
+            dma((7,)),
             dma((3,)),
             dma((3,)),
             dma((CHUNKS, members)),
@@ -490,7 +521,7 @@
             dma((CHUNKS, zn)),
         ],
         compiler_params=pltpu.CompilerParams(
-            collective_id=0, has_side_effects=True, vmem_limit_bytes=40 * 2**20
+            collective_id=0, has_side_effects=True, vmem_limit_bytes=48 * 2**20
         ),
         cost_estimate=pl.CostEstimate(
             flops=2 * members * tokens * slab * width, bytes_accessed=6 * 2**20, transcendentals=0

time: 94.7 us -> 91.5 us (0.966)
  the two profiles are of different devices: /device:TPU:24 before, /device:TPU:0 now
where the time goes in v2:
time: 91.5 us; the launch traced here: 91.1 us
  Pallas kernels  81.4 us (89%)
  local copies, waits for them, and re-layouts  9.05 us (10%)
    pallas_call x1, Pallas kernels, fused(): pl.pallas_call(functools.partial(kernel, d_model), out_shape=(jax.ShapeDt...  81.4 us
    unnamed x17, local copies, waits for them, and re-layouts  9.05 us

profile of v2, /device:TPU:0, one launch (start us, length us, event | category | flops | bytes accessed | tf_op | source)
XLA Modules:
  0.0 91.1 jit_solution(16696326776938516854)
XLA Ops:
  0.6 0.0 copy-start
  0.6 1.6 %copy-done = bf16[1024,1024]{1,0:T(8,128)(2,1)S(1)} copy-done((bf16[1024,1024]{1,0:T(8,128)(2,1)S(1)}, bf16[1024,1024]{1,0:T(8,128)(2,1)}, u32[]{:S(2)}) %copy-start) | copy-done | bytes 2097176
  2.2 0.0 copy-start.1
  2.2 1.2 %copy-done.1 = bf16[128,4096]{1,0:T(8,128)(2,1)S(1)} copy-done((bf16[128,4096]{1,0:T(8,128)(2,1)S(1)}, bf16[128,4096]{1,0:T(8,128)(2,1)}, u32[]{:S(2)}) %copy-start.1) | copy-done | bytes 1048600
  3.5 0.0 copy-start.2
  3.5 0.9 %copy-done.2 = bf16[128,1024]{1,0:T(8,128)(2,1)S(1)} copy-done((bf16[128,1024]{1,0:T(8,128)(2,1)S(1)}, bf16[128,1024]{1,0:T(8,128)(2,1)}, u32[]{:S(2)}) %copy-start.2) | copy-done | bytes 262168
  4.4 0.0 copy-start.3
  4.4 0.7 copy-done.3
  5.1 0.0 copy-start.4
  5.1 0.7 copy-done.4
  5.8 0.0 copy-start.5
  5.8 0.7 copy-done.5
  6.5 0.0 copy-start.6
  6.5 0.7 copy-done.6
  7.2 81.4 %shard_map.94 = (bf16[1024,1024]{1,0:T(8,128)(2,1)S(1)}, f32[16,86]{1,0:T(8,128)S(1)}, f32[8,128]{1,0:T(8,128)S(1)}) custom-call(bf16[128,4096]{1,0:T(8,128)(2,1)S(1)} %copy-done.1, bf16[128,1024]{1,0:T(8,128)(2,1)S(1)} %copy-done.2, f32[1,4096]{1,0:T(1,128)S(1)} %bitcast.9, bf16[1024,1024]{1,0:T(8,128)(2,1)S(1)} %copy-done, f32[16,86]{1,0:T(8,128)S(1)} %bitcast.10, ...), custom_call_target="tpu_custom_call" | custom-call | flops 1073741824 | bytes 6291456 | tf_op jit(solution)/shard_map/pallas_call | solution.py:472
  88.6 1.3 %copy.13 = bf16[1024,1024]{1,0:T(8,128)(2,1)} copy(bf16[1024,1024]{1,0:T(8,128)(2,1)S(1)} %get-tuple-element.12) | data formatting | bytes 4194304
  89.9 0.6 copy.14
  90.5 0.6 copy.15
Async XLA Ops:
  0.6 1.6 %copy-start = (bf16[1024,1024]{1,0:T(8,128)(2,1)S(1)}, bf16[1024,1024]{1,0:T(8,128)(2,1)}, u32[]{:S(2)}) copy-start(bf16[1024,1024]{1,0:T(8,128)(2,1)} %weights.1) | copy-start | bytes 6291460
  2.2 1.2 %copy-start.1 = (bf16[128,4096]{1,0:T(8,128)(2,1)S(1)}, bf16[128,4096]{1,0:T(8,128)(2,1)}, u32[]{:S(2)}) copy-start(bf16[128,4096]{1,0:T(8,128)(2,1)} %normed.1) | copy-start | bytes 3145732
  3.5 0.9 %copy-start.2 = (bf16[128,1024]{1,0:T(8,128)(2,1)S(1)}, bf16[128,1024]{1,0:T(8,128)(2,1)}, u32[]{:S(2)}) copy-start(bf16[128,1024]{1,0:T(8,128)(2,1)} %cot.1) | copy-start | bytes 786436
  4.4 0.7 copy-start.3
  5.1 0.7 copy-start.4
  5.8 0.7 copy-start.5
  6.5 0.7 copy-start.6

commit v3 on v2

--- a/solution.py
+++ b/solution.py
@@ -210,7 +210,7 @@
         pltpu.make_async_copy(state_in, state, local_sem.at[0]),
         pltpu.make_async_copy(owner_in, owner, local_sem.at[1]),
         pltpu.make_async_copy(cot, c_all.at[i], local_sem.at[2]),
-        pltpu.make_async_copy(normed.at[:, slab_at], x_all.at[0], local_sem.at[3]),
+        pltpu.make_async_copy(normed.at[:, slab_at], x_all.at[i], local_sem.at[3]),
         pltpu.make_async_copy(gain_in.at[:, slab_at], gain, local_sem.at[4]),
         pltpu.make_async_copy(col_in, col_state, local_sem.at[5]),
         pltpu.make_async_copy(weights, w_all, local_sem.at[6]),
@@ -233,7 +233,7 @@
             to = intra_peer(d)
             x_copies[k, d] = remote(
                 normed.at[:, pl.ds(pl.multiple_of(to * slab + k * step, step), step)],
-                x_all.at[d, :, pl.ds(k * step, step)],
+                x_all.at[i, :, pl.ds(k * step, step)],
                 xs.at[k, d],
                 xr.at[k, d],
                 (g, to),
@@ -305,15 +305,14 @@
         for d in range(1, members):
             x_copies[k, d].wait_recv()
         gains = gain[:, rows(k)]
-        total = jnp.zeros((step, cot.shape[1]), jnp.float32)
-        for d in range(members):
-            scaled = (x_all[d, :, rows(k)].astype(jnp.float32) * gains).astype(jnp.bfloat16)
-            total = total + lax.dot_general(
-                scaled,
-                c_all[lax.rem(i + members - d, members)],
-                (((0,), (0,)), ((), ())),
-                preferred_element_type=jnp.float32,
-            )
+        depth = members * cot.shape[0]
+        scaled = (x_all[:, :, rows(k)].reshape(depth, step).astype(jnp.float32) * gains).astype(jnp.bfloat16)
+        total = lax.dot_general(
+            scaled,
+            c_all[...].reshape(depth, cot.shape[1]),
+            (((0,), (0,)), ((), ())),
+            preferred_element_type=jnp.float32,
+        )
         total = total.astype(jnp.bfloat16)
         for t in range(groups):
             part[t // 2, t % 2, rows(k), :] = total[:, t * head : (t + 1) * head]
@@ -521,7 +520,7 @@
             dma((CHUNKS, zn)),
         ],
         compiler_params=pltpu.CompilerParams(
-            collective_id=0, has_side_effects=True, vmem_limit_bytes=48 * 2**20
+            collective_id=0, has_side_effects=True, vmem_limit_bytes=62 * 2**20
         ),
         cost_estimate=pl.CostEstimate(
             flops=2 * members * tokens * slab * width, bytes_accessed=6 * 2**20, transcendentals=0

time: 91.5 us -> 88.1 us (0.963)
  local copies, waits for them, and re-layouts: 9.05 us -> 4.28 us
  Pallas kernels: 81.4 us -> 82.8 us
    unnamed x17 -> x7, local copies, waits for them, and re-layouts: 9.05 us -> 4.28 us
    pallas_call x1, Pallas kernels: 81.4 us -> 82.8 us  [fused(): pl.pallas_call(functools.partial(kernel, d_model), out_shape=(jax.ShapeDt...]
where the time goes in v3:
time: 88.1 us; the launch traced here: 87.8 us
  Pallas kernels  82.8 us (94%)
  local copies, waits for them, and re-layouts  4.28 us (5%)
    pallas_call x1, Pallas kernels, fused(): pl.pallas_call(functools.partial(kernel, d_model), out_shape=(jax.ShapeDt...  82.8 us
    unnamed x7, local copies, waits for them, and re-layouts  4.28 us

profile of v3, /device:TPU:0, one launch (start us, length us, event | category | flops | bytes accessed | tf_op | source)
XLA Modules:
  0.0 87.8 jit_solution(15926807143083205249)
XLA Ops:
  0.6 82.8 %shard_map.94 = (bf16[1024,1024]{1,0:T(8,128)(2,1)}, f32[16,86]{1,0:T(8,128)}, f32[8,128]{1,0:T(8,128)}) custom-call(bf16[128,4096]{1,0:T(8,128)(2,1)} %normed.1, bf16[128,1024]{1,0:T(8,128)(2,1)} %cot.1, f32[1,4096]{1,0:T(1,128)} %bitcast.9, bf16[1024,1024]{1,0:T(8,128)(2,1)} %weights.1, f32[16,86]{1,0:T(8,128)} %bitcast.10, f32[8,128]{1,0:T(8,128)} %col_in.1, ...), custom_call_target="tpu_custom_call" | custom-call | flops 1073741824 | bytes 6291456 | tf_op jit(solution)/shard_map/pallas_call | solution.py:471
  83.5 0.0 copy-start
  83.5 0.0 copy-start.1
  83.5 3.1 %copy.13 = bf16[1024,1024]{1,0:T(8,128)(2,1)} copy(bf16[1024,1024]{1,0:T(8,128)(2,1)} %get-tuple-element.12) | data formatting | bytes 4194304
  86.6 0.0 copy-done
  86.6 0.6 copy.14
  87.2 0.0 copy-done.1
  87.2 0.6 copy.15
Async XLA Ops:
  83.5 3.1 %copy-start = (f32[16,86]{1,0:T(8,128)S(1)}, f32[16,86]{1,0:T(8,128)}, u32[]{:S(2)}) copy-start(f32[16,86]{1,0:T(8,128)} %get-tuple-element.7) | copy-start | bytes 16516
  83.5 3.7 %copy-start.1 = (f32[8,128]{1,0:T(8,128)S(1)}, f32[8,128]{1,0:T(8,128)}, u32[]{:S(2)}) copy-start(f32[8,128]{1,0:T(8,128)} %get-tuple-element.14) | copy-start | bytes 12292
